TPU v7x, 32 devices: a whole 2x2x4 slice. The times are simulated.
32 devices in a mesh: elem: 4 (over y, core), col: 4 (over z), pole: 2 (over x).
Axes of the slice: x: 2, y: 2, z: 4, core: 2. Of those that a mesh axis runs over, the one named last changes fastest.
Arguments:
- basis_seed: bfloat16 [4, 16, 4, 16, 384], P('elem', 'pole', 'col'), may hold values from -6 to 6
- potential: bfloat16 [4, 16, 256], P('elem'), may hold values from 0 to 2
Outputs:
- diag_blocks: float32 [4, 96, 96], P('elem', 'col')
- coupling_blocks: float32 [4, 2, 96, 96], P('elem', None, 'col')
All inputs are finite; a program needn't handle non-finite values.
Results may differ from a plain program's by a relative error of at most 0.0041.
Values may be sent and summed in bfloat16 or wider, within the bound.
A program may use at most 64 MiB of HBM per device.

v0:
```python
import jax
import jax.numpy as jnp
from jax import lax
from jax.sharding import PartitionSpec as P

C = 12
DEG = 4
PASSES = 2


filter_center = 5.5
filter_half = 4.5
penalty = 2.0


def extended(block, sides, width):
    for axis, dim in sides:
        count = lax.axis_size(axis)
        forward = [(i, i + 1) for i in range(count - 1)]
        forward.append((count - 1, 0))
        backward = [(target, source) for source, target in forward]
        low = lax.ppermute(
            lax.slice_in_dim(block, block.shape[dim] - width, None, axis=dim), axis, forward
        )
        high = lax.ppermute(lax.slice_in_dim(block, 0, width, axis=dim), axis, backward)
        block = jnp.concatenate([low, block, high], axis=dim)
    return block


def swapped(block, axis, apart):
    count = lax.axis_size(axis)
    route = []
    for low in range(count):
        high = low | 1 << apart
        if high != low and high < count:
            route += [(low, high), (high, low)]
    return lax.ppermute(block, axis, route)


def shifted(shard, axis, by):
    count = lax.axis_size(axis)
    return lax.ppermute(shard, axis, [(i, (i + by) % count) for i in range(count)])


def operation_kinds():
    step_kinds = []
    for pass_index in range(PASSES):
        step_kinds = step_kinds + ["first"] + ["later"] * (DEG - 1)
    return step_kinds + ["plain"]


def box_rows(pot_box, x_rows, extent):
    picked = jnp.take(pot_box, x_rows % extent, axis=0).astype(jnp.float32)
    return picked.reshape(x_rows.shape[0], extent, extent)


def apply_hamiltonian(padded, pot_cells, stride):
    center = padded[2:-2]
    second_x = (
        -padded[:-4] + 16.0 * padded[1:-3] - 30.0 * center + 16.0 * padded[3:-1] - padded[4:]
    ) / 12.0
    second_z = (
        -jnp.roll(center, 2, 1)
        + 16.0 * jnp.roll(center, 1, 1)
        - 30.0 * center
        + 16.0 * jnp.roll(center, -1, 1)
        - jnp.roll(center, -2, 1)
    ) / 12.0
    second_y = (
        -jnp.roll(center, 2 * stride, 2)
        + 16.0 * jnp.roll(center, stride, 2)
        - 30.0 * center
        + 16.0 * jnp.roll(center, -stride, 2)
        - jnp.roll(center, -2 * stride, 2)
    ) / 12.0
    return -0.5 * (second_x + second_z + second_y) + pot_cells * center


def first_step(applied, current):
    return (applied - filter_center * current) / filter_half


def later_step(applied, current, previous):
    return 2.0 / filter_half * (applied - filter_center * current) - previous


def expand_potential(pot_box, width_dev):
    return jnp.repeat(pot_box, width_dev, axis=2)


def slope_of(upper_layer, lower_layer):
    return (upper_layer.astype(jnp.float32) - lower_layer.astype(jnp.float32)).astype(jnp.bfloat16)


def face_block(product, left_side, base):
    top_trace, top_slope, bottom_trace, bottom_slope = left_side
    return (
        penalty * (product(top_trace, base) + product(bottom_trace, base + 2))
        - 0.25 * (product(top_slope, base) + product(top_trace, base + 1))
        + 0.25 * (product(bottom_slope, base + 2) + product(bottom_trace, base + 3))
    )


def couple_block(product, left_side, base):
    top_trace, top_slope = left_side
    return (
        0.25 * product(top_slope, base)
        - 0.25 * product(top_trace, base + 1)
        - penalty * product(top_trace, base)
    )


def local(basis_seed, potential):
    seed_box = basis_seed[0, :, 0]
    rows_dev, extent, lanes = seed_box.shape
    width_dev = lanes // extent
    pole_index = lax.axis_index("pole")
    pot_box = potential[0]
    own_rows = pole_index * rows_dev + jnp.arange(rows_dev, dtype=jnp.int32)
    potential_own = expand_potential(box_rows(pot_box, own_rows, extent), width_dev)
    current = seed_box.astype(jnp.float32)
    step_kinds = operation_kinds()
    wide_rows = pole_index * rows_dev - 2 + jnp.arange(rows_dev + 4, dtype=jnp.int32)
    potential_wide = expand_potential(box_rows(pot_box, wide_rows, extent), width_dev)
    padded = extended(current.astype(jnp.bfloat16), (("pole", 0),), 2).astype(current.dtype)
    applied = apply_hamiltonian(padded, potential_own, width_dev)
    previous, current = (current, first_step(applied, current))
    for pair_index in range(len(step_kinds) // 2):
        second_kind = step_kinds[2 * pair_index + 2]
        deep_now, deep_before = (
            extended(current, (("pole", 0),), 4),
            extended(previous, (("pole", 0),), 4),
        )
        applied = apply_hamiltonian(deep_now, potential_wide, width_dev)
        wide_now = deep_now[2:-2]
        wide_fresh = later_step(applied, wide_now, deep_before[2:-2])
        if second_kind == "plain":
            basis_wide = wide_fresh.astype(jnp.bfloat16)
            rounded = lax.optimization_barrier(basis_wide).astype(jnp.float32)
            imaged = apply_hamiltonian(rounded, potential_own, width_dev).astype(jnp.bfloat16)
            basis_cells = basis_wide[2:-2]
        else:
            applied = apply_hamiltonian(wide_fresh, potential_own, width_dev)
            inner_now = wide_fresh[2:-2]
            if second_kind == "first":
                fresh_iter = first_step(applied, inner_now)
            else:
                fresh_iter = later_step(applied, inner_now, wide_now[2:-2])
            previous, current = (inner_now, fresh_iter)
    cells_box = basis_cells.reshape(rows_dev, extent, extent, width_dev)

    def y_face(layer_index):
        return cells_box[:, :C, layer_index]

    def z_face(layer_index):
        return cells_box[:, layer_index, :C]

    own_traces = []
    for face_of in (y_face, z_face):
        top_trace = face_of(C - 1)
        bottom_trace = face_of(0)
        own_traces = own_traces + [
            top_trace,
            slope_of(top_trace, face_of(C - 2)),
            bottom_trace,
            slope_of(face_of(1), bottom_trace),
        ]
    side_next = swapped(jnp.stack([own_traces[2], own_traces[3]]), "elem", 0)
    end_next = shifted(jnp.stack([own_traces[6], own_traces[7]]), "elem", -2)
    right_traces = jnp.concatenate([jnp.stack(own_traces), side_next, end_next], 0).reshape(
        1, 12, rows_dev * C * width_dev
    )
    right_cells = imaged.reshape(rows_dev, extent, extent, width_dev)[:, :C, :C].reshape(
        1, rows_dev * C * C * width_dev
    )
    row_mask = (own_rows < C).astype(jnp.bfloat16)
    left_cells = cells_box[:, :C, :C] * row_mask[:, None, None, None]
    left_traces = [trace_rows * row_mask[:, None, None] for trace_rows in own_traces]
    vol_weight = 1.0 / (C * C * C)
    face_weight = 1.0 / (C * C)
    image_piece = lax.all_gather(right_cells, "col", axis=0, tiled=True)
    trace_piece = lax.all_gather(right_traces, "col", axis=0, tiled=True)
    piece_count = image_piece.shape[0]
    right_box = image_piece.reshape(piece_count, rows_dev, C, C, width_dev)
    right_faces = trace_piece.reshape(piece_count, 12, rows_dev, C, width_dev)

    def product(left_side, trace_index):
        return jnp.einsum(
            "abp,kabq->pkq",
            left_side,
            right_faces[:, trace_index],
            preferred_element_type=jnp.float32,
        ).reshape(width_dev, piece_count * width_dev)

    volume = jnp.einsum(
        "abcp,kabcq->pkq", left_cells, right_box, preferred_element_type=jnp.float32
    ).reshape(width_dev, piece_count * width_dev)
    diag_part = vol_weight * volume + face_weight * (
        face_block(product, left_traces[0:4], 0) + face_block(product, left_traces[4:8], 4)
    )
    coupling_part = face_weight * jnp.stack(
        [couple_block(product, left_traces[0:2], 8), couple_block(product, left_traces[4:6], 10)]
    )
    diag_full, coupling_full = lax.psum((diag_part, coupling_part), "pole")
    return (diag_full[None], coupling_full[None])


def solution(mesh):
    placed = (P("elem", "pole", "col", None, None), P("elem", None, None))
    return jax.shard_map(
        local,
        mesh=mesh,
        in_specs=placed,
        out_specs=(P("elem", "col", None), P("elem", None, "col", None)),
        check_vma=False,
    )
```

profile of v0, /device:TPU:0, one launch (start us, length us, event | category | flops | bytes accessed | tf_op | source)
XLA Modules:
  0.0 115.3 jit_solution(12530436728830713065)
XLA Ops:
  0.6 0.8 slice_bitcast_fusion.18
  1.4 2.9 %collective-permute-start = (bf16[2,16,384]{2,1,0:T(8,128)(2,1)S(1)}, bf16[2,16,384]{2,1,0:T(8,128)(2,1)S(1)}, u32[]{:S(2)}, u32[]{:S(2)}) collective-permute-start(bf16[2,16,384]{2,1,0:T(8,128)(2,1)S(1)} %get-tuple-element.179), channel_id=1, source_target_pairs={{0,1},{1,0},{2,3},{3,2},{4,5},{5,4},{6,7},{7,6},{8,9},{9,8},{10,11... | collective-permute-start | bytes 73736 | tf_op jit(solution)/shard_map/ppermute | solution.py:22
  4.4 0.9 bitcast_convert_fusion
  5.4 2.0 %collective-permute-start.4 = (f32[4,16,384]{2,1,0:T(8,128)S(1)}, f32[4,16,384]{2,1,0:T(8,128)S(1)}, u32[]{:S(2)}, u32[]{:S(2)}) collective-permute-start(f32[4,16,384]{2,1,0:T(8,128)S(1)} %get-tuple-element.159), channel_id=1, source_target_pairs={{0,1},{1,0},{2,3},{3,2},{4,5},{5,4},{6,7},{7,6},{8,9},{9,8},{10,11... | collective-permute-start | bytes 294920 | tf_op jit(solution)/shard_map/ppermute | solution.py:22
  7.5 0.6 compare_convert_fusion
  8.1 0.6 gather_fusion
  9.2 0.5 reshape.402
  9.7 0.6 gather_fusion.1
  11.4 2.0 %collective-permute-start.2 = (f32[4,16,384]{2,1,0:T(8,128)S(1)}, f32[4,16,384]{2,1,0:T(8,128)S(1)}, u32[]{:S(2)}, u32[]{:S(2)}) collective-permute-start(f32[4,16,384]{2,1,0:T(8,128)S(1)} %get-tuple-element.157), channel_id=1, source_target_pairs={{0,1},{1,0},{2,3},{3,2},{4,5},{5,4},{6,7},{7,6},{8,9},{9,8},{10,11... | collective-permute-start | bytes 294920 | tf_op jit(solution)/shard_map/ppermute | solution.py:22
  13.6 0.5 broadcast_in_dim.46
  14.1 0.8 reshape.403
  14.9 1.7 %collective-permute-done.2 = f32[4,16,384]{2,1,0:T(8,128)S(1)} collective-permute-done((f32[4,16,384]{2,1,0:T(8,128)S(1)}, f32[4,16,384]{2,1,0:T(8,128)S(1)}, u32[]{:S(2)}, u32[]{:S(2)}) %collective-permute-start.2) | collective-permute-done | bytes 98336 | tf_op jit(solution)/shard_map/ppermute | solution.py:22
  16.6 1.5 %collective-permute-done.3 = f32[4,16,384]{2,1,0:T(8,128)S(1)} collective-permute-done((f32[4,16,384]{2,1,0:T(8,128)S(1)}, f32[4,16,384]{2,1,0:T(8,128)S(1)}, u32[]{:S(2)}, u32[]{:S(2)}) %collective-permute-start.3) | collective-permute-done | bytes 98336 | tf_op jit(solution)/shard_map/ppermute | solution.py:25
  18.7 0.6 fusion.91
  20.2 1.1 collective-permute-start.6
  21.4 1.0 collective-permute-start.7
  22.4 1.1 collective-permute-start.8
  23.5 1.0 collective-permute-start.9
  24.4 1.6 %collective-permute-done.6 = f32[4,16,384]{2,1,0:T(8,128)S(1)} collective-permute-done((f32[4,16,384]{2,1,0:T(8,128)S(1)}, f32[4,16,384]{2,1,0:T(8,128)S(1)}, u32[]{:S(2)}, u32[]{:S(2)}) %collective-permute-start.6) | collective-permute-done | bytes 98336 | tf_op jit(solution)/shard_map/ppermute | solution.py:22
  26.0 1.3 %collective-permute-done.7 = f32[4,16,384]{2,1,0:T(8,128)S(1)} collective-permute-done((f32[4,16,384]{2,1,0:T(8,128)S(1)}, f32[4,16,384]{2,1,0:T(8,128)S(1)}, u32[]{:S(2)}, u32[]{:S(2)}) %collective-permute-start.7) | collective-permute-done | bytes 98336 | tf_op jit(solution)/shard_map/ppermute | solution.py:25
  27.9 0.4 collective-permute-done.8
  28.4 1.1 collective-permute-done.9
  29.4 0.6 fusion.72
  30.9 0.8 collective-permute-start.10
  31.7 1.3 %collective-permute-start.11 = (f32[4,16,384]{2,1,0:T(8,128)S(1)}, f32[4,16,384]{2,1,0:T(8,128)S(1)}, u32[]{:S(2)}, u32[]{:S(2)}) collective-permute-start(f32[4,16,384]{2,1,0:T(8,128)S(1)} %get-tuple-element.154), channel_id=1, source_target_pairs={{1,0},{0,1},{3,2},{2,3},{5,4},{4,5},{7,6},{6,7},{9,8},{8,9},{11,10... | collective-permute-start | bytes 294920 | tf_op jit(solution)/shard_map/ppermute | solution.py:25
  33.0 0.8 collective-permute-start.12
  33.8 1.3 %collective-permute-start.13 = (f32[4,16,384]{2,1,0:T(8,128)S(1)}, f32[4,16,384]{2,1,0:T(8,128)S(1)}, u32[]{:S(2)}, u32[]{:S(2)}) collective-permute-start(f32[4,16,384]{2,1,0:T(8,128)S(1)} %get-tuple-element.118), channel_id=1, source_target_pairs={{1,0},{0,1},{3,2},{2,3},{5,4},{4,5},{7,6},{6,7},{9,8},{8,9},{11,10... | collective-permute-start | bytes 294920 | tf_op jit(solution)/shard_map/ppermute | solution.py:25
  35.1 0.9 collective-permute-done.10
  36.0 1.1 collective-permute-done.11
  37.7 0.4 collective-permute-done.12
  38.1 1.1 collective-permute-done.13
  39.2 0.5 fusion.53
  40.3 0.4 fusion.140
  40.7 0.8 collective-permute-start.14
  41.5 1.3 %collective-permute-start.15 = (f32[4,16,384]{2,1,0:T(8,128)S(1)}, f32[4,16,384]{2,1,0:T(8,128)S(1)}, u32[]{:S(2)}, u32[]{:S(2)}) collective-permute-start(f32[4,16,384]{2,1,0:T(8,128)S(1)} %get-tuple-element.152), channel_id=1, source_target_pairs={{1,0},{0,1},{3,2},{2,3},{5,4},{4,5},{7,6},{6,7},{9,8},{8,9},{11,10... | collective-permute-start | bytes 294920 | tf_op jit(solution)/shard_map/ppermute | solution.py:25
  42.8 0.8 collective-permute-start.16
  43.6 1.3 %collective-permute-start.17 = (f32[4,16,384]{2,1,0:T(8,128)S(1)}, f32[4,16,384]{2,1,0:T(8,128)S(1)}, u32[]{:S(2)}, u32[]{:S(2)}) collective-permute-start(f32[4,16,384]{2,1,0:T(8,128)S(1)} %get-tuple-element.100), channel_id=1, source_target_pairs={{1,0},{0,1},{3,2},{2,3},{5,4},{4,5},{7,6},{6,7},{9,8},{8,9},{11,10... | collective-permute-start | bytes 294920 | tf_op jit(solution)/shard_map/ppermute | solution.py:25
  44.9 0.5 collective-permute-done.14
  45.4 1.1 collective-permute-done.15
  47.1 0.4 collective-permute-done.16
  47.5 1.1 collective-permute-done.17
  48.6 0.6 fusion.34
  49.1 0.7 reshape.404
  50.5 0.6 fusion.352
  51.2 0.6 pad_maximum_fusion.29
  51.8 1.3 %collective-permute-start.19 = (bf16[2,8,12,24]{3,2,1,0:T(8,128)(2,1)}, bf16[2,8,12,24]{3,2,1,0:T(8,128)(2,1)S(1)}, u32[]{:S(2)}, u32[]{:S(2)}) collective-permute-start(bf16[2,8,12,24]{3,2,1,0:T(8,128)(2,1)} %pad_maximum_fusion.29), channel_id=1, source_target_pairs={{0,16},{8,24},{16,0},{24,8},{1,17},{9,25},{17,1},{25,9},{2,18},{10... | collective-permute-start | bytes 27656 | tf_op jit(solution)/shard_map/ppermute | solution.py:42
  53.3 0.6 pad_maximum_fusion.28
  54.0 0.7 reshape.412
  55.5 0.5 copy-done.10
  56.0 1.1 fusion.130
  57.1 0.7 reshape.405
  57.8 0.4 reshape.431
  58.3 15.6 %all-gather = bf16[4,1,27648]{2,1,0:T(2,128)(2,1)S(1)} all-gather(bf16[1,1,27648]{2,1,0:T(2,128)(2,1)S(1)} %reshape.431), channel_id=1, replica_groups=mesh['elem'=4,'col'=4,'pole'=2] {'col'}, dimensions={0}, use_global_device_ids=true | all-gather | bytes 276480 | tf_op jit(solution)/shard_map/all_gather | solution.py:181
  73.9 1.4 %reduce = bf16[4,27648]{1,0:T(4,128)(2,1)S(1)} reduce(bf16[4,1,27648]{2,1,0:T(2,128)(2,1)S(1)} %all-gather, bf16[]{:T(256)} %constant.124), dimensions={1}, to_apply=%all-gather.reduce_sub_computation | reduce | bytes 442370 | tf_op jit(solution)/shard_map/all_gather | solution.py:181
  75.4 1.8 %reshape.407 = bf16[4,8,12,12,24]{4,3,2,1,0:T(8,128)(2,1)S(1)} reshape(bf16[4,27648]{1,0:T(4,128)(2,1)S(1)} %reduce) | data formatting | bytes 442368 | tf_op jit(solution)/shard_map/reshape | solution.py:184
  77.1 1.5 %copy.95 = bf16[4,24,8,12,12]{1,0,4,3,2:T(4,128)(2,1)S(1)} copy(bf16[4,24,8,12,12]{1,4,3,2,0:T(8,128)(2,1)S(1)} %bitcast.349) | data formatting | bytes 442368 | tf_op jit(solution)/shard_map/abcp,kabcq->pkq/dot_general | solution.py:195
  78.6 1.3 %reshape.454 = bf16[96,8,12,12]{0,3,2,1:T(8,128)(2,1)} reshape(bf16[4,24,8,12,12]{1,0,4,3,2:T(4,128)(2,1)S(1)} %copy.95) | data formatting | bytes 442368 | tf_op jit(solution)/shard_map/abcp,kabcq->pkq/dot_general | solution.py:195
  80.4 14.4 %all_gather.7 = bf16[4,12,2304]{2,1,0:T(8,128)(2,1)S(1)} all-gather(bf16[1,12,2304]{2,1,0:T(8,128)(2,1)S(1)} %concatenate.394), channel_id=1, replica_groups=mesh['elem'=4,'col'=4,'pole'=2] {'col'}, dimensions={0}, use_global_device_ids=true | all-gather | bytes 276480 | tf_op jit(solution)/shard_map/all_gather | solution.py:182
  94.9 1.8 %reshape.408 = bf16[4,12,8,12,24]{4,3,2,0,1:T(8,128)(2,1)S(1)} reshape(bf16[4,12,2304]{2,0,1:T(4,128)(2,1)S(1)} %copy.63) | data formatting | bytes 442368 | tf_op jit(solution)/shard_map/reshape | solution.py:185
  96.7 0.5 slice_bitcast_fusion.2
  97.6 1.1 fusion.11
  98.7 1.0 fusion.10
  99.7 1.0 fusion.8
  106.8 8.5 %all-reduce = (f32[1,24,96]{2,1,0:T(8,128)}, f32[1,2,24,96]{3,2,1,0:T(8,128)}) all-reduce(f32[1,24,96]{2,1,0:T(8,128)S(1)} %fusion.14, f32[1,2,24,96]{3,2,1,0:T(8,128)S(1)} %fusion.244), channel_id=1, replica_groups=mesh['elem'=4,'col'=4,'pole'=2] {'pole'}, use_global_device_ids=true, to_apply=%region_0.1 | all-reduce | flops 6912 | bytes 55296 | tf_op jit(solution)/shard_map/psum | solution.py:204
  (206 shorter events, 15.0 us)
Async XLA Ops:
  0.6 7.4 %copy-start = (bf16[1,16,256]{2,1,0:T(8,128)(2,1)S(1)}, bf16[1,16,256]{2,1,0:T(8,128)(2,1)}, u32[]{:S(2)}) copy-start(bf16[1,16,256]{2,1,0:T(8,128)(2,1)} %param.3) | copy-start | bytes 24580
  1.4 9.0 %collective-permute-start = (bf16[2,16,384]{2,1,0:T(8,128)(2,1)S(1)}, bf16[2,16,384]{2,1,0:T(8,128)(2,1)S(1)}, u32[]{:S(2)}, u32[]{:S(2)}) collective-permute-start(bf16[2,16,384]{2,1,0:T(8,128)(2,1)S(1)} %get-tuple-element.179), channel_id=1, source_target_pairs={{0,1},{1,0},{2,3},{3,2},{4,5},{5,4},{6,7},{7,6},{8,9},{9,8},{10,11... | collective-permute-start | bytes 73736 | tf_op jit(solution)/shard_map/ppermute | solution.py:22
  4.4 6.1 %collective-permute-start.1 = (bf16[2,16,384]{2,1,0:T(8,128)(2,1)S(1)}, bf16[2,16,384]{2,1,0:T(8,128)(2,1)S(1)}, u32[]{:S(2)}, u32[]{:S(2)}) collective-permute-start(bf16[2,16,384]{2,1,0:T(8,128)(2,1)S(1)} %get-tuple-element.180), channel_id=1, source_target_pairs={{1,0},{0,1},{3,2},{2,3},{5,4},{4,5},{7,6},{6,7},{9,8},{8,9},{11,10... | collective-permute-start | bytes 73736 | tf_op jit(solution)/shard_map/ppermute | solution.py:25
  5.3 5.1 %copy-start.4 = (bf16[1,8,1,16,384]{4,3,2,1,0:T(8,128)(2,1)S(1)}, bf16[1,8,1,16,384]{4,3,2,1,0:T(8,128)(2,1)}, u32[]{:S(2)}) copy-start(bf16[1,8,1,16,384]{4,3,2,1,0:T(8,128)(2,1)} %param.2) | copy-start | bytes 294916
  5.4 13.3 %collective-permute-start.4 = (f32[4,16,384]{2,1,0:T(8,128)S(1)}, f32[4,16,384]{2,1,0:T(8,128)S(1)}, u32[]{:S(2)}, u32[]{:S(2)}) collective-permute-start(f32[4,16,384]{2,1,0:T(8,128)S(1)} %get-tuple-element.159), channel_id=1, source_target_pairs={{0,1},{1,0},{2,3},{3,2},{4,5},{5,4},{6,7},{7,6},{8,9},{9,8},{10,11... | collective-permute-start | bytes 294920 | tf_op jit(solution)/shard_map/ppermute | solution.py:22
  7.4 11.3 %collective-permute-start.5 = (f32[4,16,384]{2,1,0:T(8,128)S(1)}, f32[4,16,384]{2,1,0:T(8,128)S(1)}, u32[]{:S(2)}, u32[]{:S(2)}) collective-permute-start(f32[4,16,384]{2,1,0:T(8,128)S(1)} %get-tuple-element.160), channel_id=1, source_target_pairs={{1,0},{0,1},{3,2},{2,3},{5,4},{4,5},{7,6},{6,7},{9,8},{8,9},{11,10... | collective-permute-start | bytes 294920 | tf_op jit(solution)/shard_map/ppermute | solution.py:25
  11.4 5.1 %collective-permute-start.2 = (f32[4,16,384]{2,1,0:T(8,128)S(1)}, f32[4,16,384]{2,1,0:T(8,128)S(1)}, u32[]{:S(2)}, u32[]{:S(2)}) collective-permute-start(f32[4,16,384]{2,1,0:T(8,128)S(1)} %get-tuple-element.157), channel_id=1, source_target_pairs={{0,1},{1,0},{2,3},{3,2},{4,5},{5,4},{6,7},{7,6},{8,9},{9,8},{10,11... | collective-permute-start | bytes 294920 | tf_op jit(solution)/shard_map/ppermute | solution.py:22
  13.4 4.6 %collective-permute-start.3 = (f32[4,16,384]{2,1,0:T(8,128)S(1)}, f32[4,16,384]{2,1,0:T(8,128)S(1)}, u32[]{:S(2)}, u32[]{:S(2)}) collective-permute-start(f32[4,16,384]{2,1,0:T(8,128)S(1)} %get-tuple-element.158), channel_id=1, source_target_pairs={{1,0},{0,1},{3,2},{2,3},{5,4},{4,5},{7,6},{6,7},{9,8},{8,9},{11,10... | collective-permute-start | bytes 294920 | tf_op jit(solution)/shard_map/ppermute | solution.py:25
  19.3 3.1 %copy-start.2 = (f32[12,16,384]{2,1,0:T(8,128)}, f32[12,16,384]{2,1,0:T(8,128)S(1)}, u32[]{:S(2)}) copy-start(f32[12,16,384]{2,1,0:T(8,128)S(1)} %fusion.91) | copy-start | bytes 884740
  20.2 5.8 %collective-permute-start.6 = (f32[4,16,384]{2,1,0:T(8,128)S(1)}, f32[4,16,384]{2,1,0:T(8,128)S(1)}, u32[]{:S(2)}, u32[]{:S(2)}) collective-permute-start(f32[4,16,384]{2,1,0:T(8,128)S(1)} %get-tuple-element.155), channel_id=1, source_target_pairs={{0,1},{1,0},{2,3},{3,2},{4,5},{5,4},{6,7},{7,6},{8,9},{9,8},{10,11... | collective-permute-start | bytes 294920 | tf_op jit(solution)/shard_map/ppermute | solution.py:22
  21.4 5.9 %collective-permute-start.7 = (f32[4,16,384]{2,1,0:T(8,128)S(1)}, f32[4,16,384]{2,1,0:T(8,128)S(1)}, u32[]{:S(2)}, u32[]{:S(2)}) collective-permute-start(f32[4,16,384]{2,1,0:T(8,128)S(1)} %get-tuple-element.156), channel_id=1, source_target_pairs={{1,0},{0,1},{3,2},{2,3},{5,4},{4,5},{7,6},{6,7},{9,8},{8,9},{11,10... | collective-permute-start | bytes 294920 | tf_op jit(solution)/shard_map/ppermute | solution.py:25
  22.4 6.0 %collective-permute-start.8 = (f32[4,16,384]{2,1,0:T(8,128)S(1)}, f32[4,16,384]{2,1,0:T(8,128)S(1)}, u32[]{:S(2)}, u32[]{:S(2)}) collective-permute-start(f32[4,16,384]{2,1,0:T(8,128)S(1)} %get-tuple-element.135), channel_id=1, source_target_pairs={{0,1},{1,0},{2,3},{3,2},{4,5},{5,4},{6,7},{7,6},{8,9},{9,8},{10,11... | collective-permute-start | bytes 294920 | tf_op jit(solution)/shard_map/ppermute | solution.py:22
  23.5 5.9 %collective-permute-start.9 = (f32[4,16,384]{2,1,0:T(8,128)S(1)}, f32[4,16,384]{2,1,0:T(8,128)S(1)}, u32[]{:S(2)}, u32[]{:S(2)}) collective-permute-start(f32[4,16,384]{2,1,0:T(8,128)S(1)} %get-tuple-element.136), channel_id=1, source_target_pairs={{1,0},{0,1},{3,2},{2,3},{5,4},{4,5},{7,6},{6,7},{9,8},{8,9},{11,10... | collective-permute-start | bytes 294920 | tf_op jit(solution)/shard_map/ppermute | solution.py:25
  27.6 1.8 %slice-start.1 = ((f32[12,16,384]{2,1,0:T(8,128)}), f32[8,16,384]{2,1,0:T(8,128)S(1)}, s32[]{:S(2)}) async-start(f32[12,16,384]{2,1,0:T(8,128)} %copy-done.2), calls=%async_computation.1 | async-start | bytes 393216 | tf_op jit(solution)/shard_map/slice | solution.py:58
  30.0 3.1 %copy-start.1 = (f32[12,16,384]{2,1,0:T(8,128)}, f32[12,16,384]{2,1,0:T(8,128)S(1)}, u32[]{:S(2)}) copy-start(f32[12,16,384]{2,1,0:T(8,128)S(1)} %fusion.72) | copy-start | bytes 884740
  30.9 5.1 %collective-permute-start.10 = (f32[4,16,384]{2,1,0:T(8,128)S(1)}, f32[4,16,384]{2,1,0:T(8,128)S(1)}, u32[]{:S(2)}, u32[]{:S(2)}) collective-permute-start(f32[4,16,384]{2,1,0:T(8,128)S(1)} %get-tuple-element.153), channel_id=1, source_target_pairs={{0,1},{1,0},{2,3},{3,2},{4,5},{5,4},{6,7},{7,6},{8,9},{9,8},{10,11... | collective-permute-start | bytes 294920 | tf_op jit(solution)/shard_map/ppermute | solution.py:22
  31.7 5.4 %collective-permute-start.11 = (f32[4,16,384]{2,1,0:T(8,128)S(1)}, f32[4,16,384]{2,1,0:T(8,128)S(1)}, u32[]{:S(2)}, u32[]{:S(2)}) collective-permute-start(f32[4,16,384]{2,1,0:T(8,128)S(1)} %get-tuple-element.154), channel_id=1, source_target_pairs={{1,0},{0,1},{3,2},{2,3},{5,4},{4,5},{7,6},{6,7},{9,8},{8,9},{11,10... | collective-permute-start | bytes 294920 | tf_op jit(solution)/shard_map/ppermute | solution.py:25
  33.0 5.1 %collective-permute-start.12 = (f32[4,16,384]{2,1,0:T(8,128)S(1)}, f32[4,16,384]{2,1,0:T(8,128)S(1)}, u32[]{:S(2)}, u32[]{:S(2)}) collective-permute-start(f32[4,16,384]{2,1,0:T(8,128)S(1)} %get-tuple-element.117), channel_id=1, source_target_pairs={{0,1},{1,0},{2,3},{3,2},{4,5},{5,4},{6,7},{7,6},{8,9},{9,8},{10,11... | collective-permute-start | bytes 294920 | tf_op jit(solution)/shard_map/ppermute | solution.py:22
  33.8 5.4 %collective-permute-start.13 = (f32[4,16,384]{2,1,0:T(8,128)S(1)}, f32[4,16,384]{2,1,0:T(8,128)S(1)}, u32[]{:S(2)}, u32[]{:S(2)}) collective-permute-start(f32[4,16,384]{2,1,0:T(8,128)S(1)} %get-tuple-element.118), channel_id=1, source_target_pairs={{1,0},{0,1},{3,2},{2,3},{5,4},{4,5},{7,6},{6,7},{9,8},{8,9},{11,10... | collective-permute-start | bytes 294920 | tf_op jit(solution)/shard_map/ppermute | solution.py:25
  37.4 1.8 %slice-start = ((f32[12,16,384]{2,1,0:T(8,128)}), f32[8,16,384]{2,1,0:T(8,128)S(1)}, s32[]{:S(2)}) async-start(f32[12,16,384]{2,1,0:T(8,128)} %copy-done.1), calls=%async_computation | async-start | bytes 393216 | tf_op jit(solution)/shard_map/slice | solution.py:58
  39.7 3.1 %copy-start.3 = (f32[12,16,384]{2,1,0:T(8,128)}, f32[12,16,384]{2,1,0:T(8,128)S(1)}, u32[]{:S(2)}) copy-start(f32[12,16,384]{2,1,0:T(8,128)S(1)} %fusion.53) | copy-start | bytes 884740
  40.7 4.7 %collective-permute-start.14 = (f32[4,16,384]{2,1,0:T(8,128)S(1)}, f32[4,16,384]{2,1,0:T(8,128)S(1)}, u32[]{:S(2)}, u32[]{:S(2)}) collective-permute-start(f32[4,16,384]{2,1,0:T(8,128)S(1)} %get-tuple-element.151), channel_id=1, source_target_pairs={{0,1},{1,0},{2,3},{3,2},{4,5},{5,4},{6,7},{7,6},{8,9},{9,8},{10,11... | collective-permute-start | bytes 294920 | tf_op jit(solution)/shard_map/ppermute | solution.py:22
  41.5 5.0 %collective-permute-start.15 = (f32[4,16,384]{2,1,0:T(8,128)S(1)}, f32[4,16,384]{2,1,0:T(8,128)S(1)}, u32[]{:S(2)}, u32[]{:S(2)}) collective-permute-start(f32[4,16,384]{2,1,0:T(8,128)S(1)} %get-tuple-element.152), channel_id=1, source_target_pairs={{1,0},{0,1},{3,2},{2,3},{5,4},{4,5},{7,6},{6,7},{9,8},{8,9},{11,10... | collective-permute-start | bytes 294920 | tf_op jit(solution)/shard_map/ppermute | solution.py:25
  42.8 4.7 %collective-permute-start.16 = (f32[4,16,384]{2,1,0:T(8,128)S(1)}, f32[4,16,384]{2,1,0:T(8,128)S(1)}, u32[]{:S(2)}, u32[]{:S(2)}) collective-permute-start(f32[4,16,384]{2,1,0:T(8,128)S(1)} %get-tuple-element.99), channel_id=1, source_target_pairs={{0,1},{1,0},{2,3},{3,2},{4,5},{5,4},{6,7},{7,6},{8,9},{9,8},{10,11... | collective-permute-start | bytes 294920 | tf_op jit(solution)/shard_map/ppermute | solution.py:22
  43.6 5.0 %collective-permute-start.17 = (f32[4,16,384]{2,1,0:T(8,128)S(1)}, f32[4,16,384]{2,1,0:T(8,128)S(1)}, u32[]{:S(2)}, u32[]{:S(2)}) collective-permute-start(f32[4,16,384]{2,1,0:T(8,128)S(1)} %get-tuple-element.100), channel_id=1, source_target_pairs={{1,0},{0,1},{3,2},{2,3},{5,4},{4,5},{7,6},{6,7},{9,8},{8,9},{11,10... | collective-permute-start | bytes 294920 | tf_op jit(solution)/shard_map/ppermute | solution.py:25
  46.8 1.8 %slice-start.2 = ((f32[12,16,384]{2,1,0:T(8,128)}), f32[8,16,384]{2,1,0:T(8,128)S(1)}, s32[]{:S(2)}) async-start(f32[12,16,384]{2,1,0:T(8,128)} %copy-done.3), calls=%async_computation.2 | async-start | bytes 393216 | tf_op jit(solution)/shard_map/slice | solution.py:58
  50.0 3.1 %copy-start.5 = (bf16[8,12,1,24]{3,2,1,0:T(2,128)(2,1)}, bf16[8,12,1,24]{3,2,1,0:T(2,128)(2,1)S(1)}, u32[]{:S(2)}) copy-start(bf16[8,12,1,24]{3,2,1,0:T(2,128)(2,1)S(1)} %get-tuple-element.24) | copy-start | bytes 13828
  50.0 5.0 %copy-start.12 = (bf16[8,12,1,24]{3,2,1,0:T(2,128)(2,1)}, bf16[8,12,1,24]{3,2,1,0:T(2,128)(2,1)S(1)}, u32[]{:S(2)}) copy-start(bf16[8,12,1,24]{3,2,1,0:T(2,128)(2,1)S(1)} %get-tuple-element.25) | copy-start | bytes 13828
  51.8 28.2 %collective-permute-start.19 = (bf16[2,8,12,24]{3,2,1,0:T(8,128)(2,1)}, bf16[2,8,12,24]{3,2,1,0:T(8,128)(2,1)S(1)}, u32[]{:S(2)}, u32[]{:S(2)}) collective-permute-start(bf16[2,8,12,24]{3,2,1,0:T(8,128)(2,1)} %pad_maximum_fusion.29), channel_id=1, source_target_pairs={{0,16},{8,24},{16,0},{24,8},{1,17},{9,25},{17,1},{25,9},{2,18},{10... | collective-permute-start | bytes 27656 | tf_op jit(solution)/shard_map/ppermute | solution.py:42
  53.2 2.4 %copy-start.8 = (bf16[8,12,1,24]{3,1,0,2:T(8,128)(2,1)}, bf16[8,12,1,24]{3,1,0,2:T(8,128)(2,1)S(1)}, u32[]{:S(2)}) copy-start(bf16[8,12,1,24]{3,1,0,2:T(8,128)(2,1)S(1)} %get-tuple-element.5) | copy-start | bytes 13828
  53.9 26.2 %collective-permute-start.18 = (bf16[2,8,12,24]{3,2,1,0:T(8,128)(2,1)}, bf16[2,8,12,24]{3,2,1,0:T(8,128)(2,1)S(1)}, u32[]{:S(2)}, u32[]{:S(2)}) collective-permute-start(bf16[2,8,12,24]{3,2,1,0:T(8,128)(2,1)} %pad_maximum_fusion.28), channel_id=1, source_target_pairs={{0,8},{8,0},{16,24},{24,16},{1,9},{9,1},{17,25},{25,17},{2,10},{10... | collective-permute-start | bytes 27656 | tf_op jit(solution)/shard_map/ppermute | solution.py:37
  55.4 0.6 copy-start.10
  57.1 1.1 copy-start.14
  96.7 0.9 copy-start.15
  97.2 4.9 %copy-start.9 = (bf16[8,12,1,24]{3,1,0,2:T(8,128)(2,1)S(1)}, bf16[8,12,1,24]{3,1,0,2:T(8,128)(2,1)}, u32[]{:S(2)}) copy-start(bf16[8,12,1,24]{3,1,0,2:T(8,128)(2,1)} %copy-done.8) | copy-start | bytes 13828
  97.2 5.3 %copy-start.11 = (bf16[8,12,1,24]{3,1,0,2:T(8,128)(2,1)S(1)}, bf16[8,12,1,24]{3,1,0,2:T(8,128)(2,1)}, u32[]{:S(2)}) copy-start(bf16[8,12,1,24]{3,1,0,2:T(8,128)(2,1)} %copy-done.10) | copy-start | bytes 13828
  98.7 4.7 %copy-start.6 = (bf16[8,12,1,24]{3,2,1,0:T(2,128)(2,1)S(1)}, bf16[8,12,1,24]{3,2,1,0:T(2,128)(2,1)}, u32[]{:S(2)}) copy-start(bf16[8,12,1,24]{3,2,1,0:T(2,128)(2,1)} %copy-done.5) | copy-start | bytes 13828
  102.5 3.0 %copy-start.13 = (bf16[8,12,1,24]{3,2,1,0:T(2,128)(2,1)S(1)}, bf16[8,12,1,24]{3,2,1,0:T(2,128)(2,1)}, u32[]{:S(2)}) copy-start(bf16[8,12,1,24]{3,2,1,0:T(2,128)(2,1)} %copy-done.12) | copy-start | bytes 13828
  103.0 3.5 %copy-start.7 = (bf16[96,8,12,12]{0,3,2,1:T(8,128)(2,1)S(1)}, bf16[96,8,12,12]{0,3,2,1:T(8,128)(2,1)}, u32[]{:S(2)}) copy-start(bf16[96,8,12,12]{0,3,2,1:T(8,128)(2,1)} %reshape.454) | copy-start | bytes 663556
where the time goes:
time: 116 us; the launch traced here: 115 us
  blocking collectives  38.5 us (33%)
  local copies, waits for them, and re-layouts  23.1 us (20%)
  starting transfers between devices  21.1 us (18%)
  waiting for transfers between devices  13.9 us (12%)
  other arithmetic  9.63 us (8%)
  matrix products  7 us (6%)
  between operations  2.09 us (2%)
    all_gather x1, blocking collectives, local(): image_piece = lax.all_gather(right_cells, 'col', axis=0, tiled=True)  15.6 us
    all_gather x1, blocking collectives, local(): trace_piece = lax.all_gather(right_traces, 'col', axis=0, tiled=True)  14.4 us
    ppermute x9, starting transfers between devices, extended(): lax.ppermute(lax.slice_in_dim(block, block.shape[dim] - width, None, axis...  12.2 us
    psum x1, blocking collectives, local(): diag_full, coupling_full = lax.psum((diag_part, coupling_part), 'pole')  8.54 us
    ppermute x9, waiting for transfers between devices, extended(): lax.ppermute(lax.slice_in_dim(block, 0, width, axis=dim), axis, backward)  8.01 us
    ppermute x9, starting transfers between devices, extended(): lax.ppermute(lax.slice_in_dim(block, 0, width, axis=dim), axis, backward)  7.53 us
    dot_general x18, matrix products, product(): jnp.einsum('abp,kabq->pkq', left_side, right_faces[:, trace_index], prefe...  6.68 us
    ppermute x9, waiting for transfers between devices, extended(): lax.ppermute(lax.slice_in_dim(block, block.shape[dim] - width, None, axis...  5.85 us
  transfers between devices with their start and end apart: 20, of which 14 were waited for; matrix products, arithmetic and copies ran while one was open for 16% of the time, Pallas kernels for 0%

commit v1 on v0

v1 whole, which is shorter than its diff:
```python
import functools

import jax
import jax.numpy as jnp
from jax import lax
from jax.experimental import pallas as pl
from jax.experimental.pallas import tpu as pltpu
from jax.sharding import PartitionSpec as P

C = 12
DEG = 4
PASSES = 2
CENTER = 5.5
HALF = 4.5

F32 = jnp.float32
BF16 = jnp.bfloat16
MESH = pl.DeviceIdType.MESH
NT = (((1,), (1,)), ((), ()))


def iota(shape, dim):
    return lax.broadcasted_iota(jnp.int32, shape, dim)


def onehot(cond, value=1.0):
    return jnp.where(cond, value, 0.0)


def dot(a, b):
    return jnp.dot(a, b, preferred_element_type=F32)


def split(a):
    hi = a.astype(BF16)
    return hi, (a - hi.astype(F32)).astype(BF16)


def dot_split(a, b):
    hi, lo = split(a)
    return dot(hi, b) + dot(lo, b)


def swap_halves(a):
    return pltpu.roll(a.reshape(-1, 8, a.shape[-1]), 4, 1).reshape(a.shape)


def kernel(n_elem, n_col, n_pole, seed_ref, pot_ref, diag_ref, coup_ref,
           xsend, xrecv, lsend, lrecv, wsend, wrecv, ysend, yrecv, zsend, zrecv,
           bsend, brecv, send_sem, recv_sem):
    _, rows_dev, _, ext, lanes = seed_ref.shape
    width = lanes // ext
    part = width // 2
    groups = part // 4
    half = ext // 2
    cells = ext * ext
    own_cells = rows_dev * ext
    rows = half * groups * 8
    packed = (C // 2) * groups * 8
    pair = 2 * groups * 8
    blocks = packed // 16

    e = lax.axis_index("elem")
    c = lax.axis_index("col")
    p = lax.axis_index("pole")
    h = lax.rem(p, 2)
    mate = p + 1 - 2 * h
    far = lax.rem(c + n_col // 2, n_col)
    near = c + 1 - 2 * lax.rem(c, 2)
    other = 1 - h
    side_e = e + 1 - 2 * lax.rem(e, 2)
    prev_e = lax.rem(e + n_elem - 2, n_elem)
    next_e = lax.rem(e + 2, n_elem)
    peers = [(e, c, mate), (e, near, p), (e, near, mate)]
    turns = [lax.rem(p + k, n_pole) for k in range(1, n_pole)]
    turned = [lax.rem(p + n_pole - k, n_pole) for k in range(1, n_pole)]

    barrier = pltpu.get_barrier_semaphore()
    greet = peers[1:] + [(e, c, turn) for turn in turns]
    greet += [(e, far, p), (side_e, c, p), (side_e, far, p),
              (prev_e, c, p), (prev_e, far, p), (next_e, c, p), (next_e, far, p)]
    for device in greet:
        pl.semaphore_signal(barrier, inc=1, device_id=device, device_id_type=MESH)

    def remote(src, dst, sem, device):
        return pltpu.make_async_remote_copy(
            src_ref=src, dst_ref=dst, send_sem=send_sem.at[sem], recv_sem=recv_sem.at[sem],
            device_id=device, device_id_type=MESH)

    seed = seed_ref[0, :, 0].reshape(own_cells, lanes)
    sel_shape = (half, groups, 8, lanes)
    row_s = iota(sel_shape, 2)
    row_col = (iota(sel_shape, 0) * width + iota(sel_shape, 1) * 4 + (row_s & 3)
               + (row_s >> 2) * (half * width))
    lane = iota(sel_shape, 3)

    def pick(which):
        sel = onehot(lane == row_col + which * part).reshape(rows, lanes).astype(BF16)
        return lax.dot_general(sel, seed, NT, preferred_element_type=F32)

    for k, turn in enumerate(turns):
        xsend[k] = pick(lax.rem(turn, 2)).astype(BF16)
    pl.semaphore_wait(barrier, len(greet))
    first_copies = [remote(xsend.at[k], xrecv.at[k], 12 + k, (e, c, turn))
                    for k, turn in enumerate(turns)]
    for copy in first_copies:
        copy.start()
    own = pick(h)

    i0, i1 = iota((cells, cells), 0), iota((cells, cells), 1)
    same_x = (i0 // ext) == (i1 // ext)
    same_z = (i0 & (ext - 1)) == (i1 & (ext - 1))
    dz = (i0 - i1) & (ext - 1)
    dx = ((i0 - i1) // ext) & (ext - 1)

    def ring(d):
        return jnp.where((d == 1) | (d == ext - 1), -16.0,
                         jnp.where((d == 2) | (d == ext - 2), 1.0,
                                   jnp.where(d == 0, 30.0, 0.0)))

    stencil = jnp.where(same_x, ring(dz), 0.0) + jnp.where(same_z, ring(dx), 0.0)
    z0, z1 = i0 & (ext - 1), i1 & (ext - 1)
    corner = ((z0 == 0) & (z1 == 0)) | ((z0 == C - 1) & (z1 == C - 1))
    edge = (((z0 + z1) == 1) | ((z0 + z1) == 2 * C - 3)) & (
        (z0 - z1 == 1) | (z1 - z0 == 1))
    face = 24.0 * C
    stencil_w = stencil + jnp.where(same_x & corner, 1.5 * face, 0.0) + jnp.where(
        same_x & edge, 0.25 * face, 0.0)
    stencil = stencil.astype(BF16)
    stencil_w = stencil_w.astype(BF16)

    r0, l0 = iota((cells, 128), 0), iota((cells, 128), 1)
    rx, rz = r0 // ext, r0 & (ext - 1)
    core = (rx < C) & (rz < C)
    target = (C - 1 - rz) * C + rx
    to_main = onehot(core & (l0 == target)).astype(BF16)
    to_rest = onehot(core & ((l0 & 15) == target - 128)).astype(BF16)
    l32 = l0 & 31
    to_next = (onehot((rx < C) & (rz == 0) & (l32 == rx), -1.5)
               + onehot((rx < C) & (rz == 1) & (l32 == rx), -0.25)
               + onehot((rx < C) & (rz == 0) & (l32 == C + rx), -0.25)).astype(BF16)
    rep0, rep1 = iota((128, 128), 0), iota((128, 128), 1)
    to_top = onehot((rep0 < 2 * C) & ((rep1 & 31) == rep0)).astype(BF16)

    pot = pot_ref[0].astype(F32)
    p_shape = (ext, ext, cells)
    pot_z = jnp.where(iota(p_shape, 2) // ext == iota(p_shape, 1), pot[:, None, :], 0.0)
    v_shape = (half, 8, cells)
    v_sel = onehot((iota(v_shape, 2) & (ext - 1)) == iota(v_shape, 0)
                   + (iota(v_shape, 1) >> 2) * half).reshape(half * 8, cells).astype(BF16)
    pot_y = lax.dot_general(v_sel, pot_z.reshape(cells, cells).astype(BF16), NT,
                            preferred_element_type=F32).reshape(half, 1, 8, cells)
    scaled = (2.0 / HALF) * (pot_y + (1.25 - CENTER))
    scaled24 = 24.0 * pot_y + 30.0
    four_d = (half, groups, 8, cells)

    for copy in first_copies:
        copy.wait()
    pieces = []
    for source in range(n_pole):
        piece = own
        for k, turn in enumerate(turned):
            piece = jnp.where(turn == source, xrecv[k].astype(F32), piece)
        pieces.append(piece)
    start = jnp.concatenate(pieces, axis=1)

    def rows_part(f4):
        ext_f = jnp.concatenate([swap_halves(f4[half - 2:]), f4, swap_halves(f4[:2])], axis=0)
        return (ext_f[:half] + ext_f[4:]) - 16.0 * (ext_f[1:half + 1] + ext_f[3:half + 3])

    current = start.reshape(four_d)
    previous = None
    scale = 2.0 / (HALF * 24.0)
    for _ in range(PASSES):
        for k in range(DEG):
            f4 = current
            mixed = dot_split(f4.reshape(rows, cells), stencil).reshape(four_d)
            fresh = scale * (mixed + rows_part(f4)) + scaled * f4
            fresh = 0.5 * fresh if k == 0 else fresh - previous
            previous, current = f4, fresh

    basis = current.reshape(rows, cells).astype(BF16)
    basis4 = basis.astype(F32).reshape(four_d)
    upper = iota((1, groups, 8, cells), 2) >= 4

    def pack_rows(a4):
        rest = jnp.where(upper, swap_halves(a4[6:8]), a4[4:6])
        return jnp.concatenate([a4[:4], rest], axis=0).reshape(packed, cells).astype(BF16)

    def pack_blocks(a, wide):
        count = 128 // wide
        n = a.shape[0] // 16
        group = iota((16, 128), 1) // wide
        out = []
        for base in range(0, n, count):
            total = None
            for b in range(base, min(base + count, n)):
                term = jnp.where(group == b - base, a[b * 16:(b + 1) * 16], 0.0)
                total = term if total is None else total + term
            out.append(total)
        return jnp.concatenate(out, axis=0).astype(BF16)

    def unpack_blocks(tiles, n, wide):
        count = 128 // wide
        group = iota((16, 128), 1) // wide
        out = []
        for b in range(n):
            tile = tiles[(b // count) * 16:(b // count + 1) * 16].astype(F32)
            out.append(jnp.where(group == b % count, tile, 0.0))
        return jnp.concatenate(out, axis=0).astype(BF16)

    core_basis = pack_rows(basis4)
    left_main = dot(core_basis, to_main).astype(BF16)
    left_rest = dot(core_basis, to_rest)
    lsend[:packed] = left_main
    lsend[packed:] = pack_blocks(left_rest, 16)
    copies = [remote(lsend, lrecv.at[k], 1 + k, peers[k]) for k in range(3)]
    for copy in copies:
        copy.start()

    low_n = basis4[0:1] * -1.5 + basis4[1:2] * -0.25
    low_s = basis4[0:1] * -0.25
    y_rows = jnp.concatenate([jnp.where(upper, swap_halves(low_s), 0.0),
                              jnp.where(upper, swap_halves(low_n), 0.0)], axis=0)
    y_rows = y_rows.reshape(pair, cells).astype(BF16)
    ysend[:pair] = dot(y_rows, to_main).astype(BF16)
    ysend[pair:] = pack_blocks(dot(y_rows, to_rest), 16)
    zsend[...] = pack_blocks(dot(core_basis, to_next), 32)
    bottom_copies = [remote(ysend, yrecv.at[1], 5, (side_e, far, p)),
                     remote(zsend, zrecv.at[1], 7, (prev_e, far, p)),
                     remote(ysend, yrecv.at[0], 6, (side_e, c, p)),
                     remote(zsend, zrecv.at[0], 8, (prev_e, c, p))]

    image = dot(basis, stencil_w).reshape(four_d) + rows_part(basis4) + scaled24 * basis4
    low, high = jnp.logical_not(upper), upper
    image = jnp.concatenate([
        image[0:1] + jnp.where(low, face * (1.5 * basis4[0:1] + 0.25 * basis4[1:2]), 0.0),
        image[1:2] + jnp.where(low, face * 0.25 * basis4[0:1], 0.0),
        image[2:3] + jnp.where(high, face * 0.25 * basis4[3:4], 0.0),
        image[3:4] + jnp.where(high, face * (1.5 * basis4[3:4] + 0.25 * basis4[2:3]), 0.0),
        image[4:]], axis=0)
    core_image = pack_rows(image)
    right_main = dot(core_image, to_main).astype(BF16)
    right_rest = pack_blocks(dot(core_image, to_rest), 16)
    wsend[:packed] = right_main
    wsend[packed:] = right_rest
    w_copy = remote(wsend, wrecv, 4, (e, far, p))
    w_copy.start()
    for copy in bottom_copies:
        copy.start()

    m0, m1 = iota((4 * pair, 2 * pair), 0), iota((4 * pair, 2 * pair), 1)
    per = groups * 8
    same_y = ((m0 // per) & 1 == (m1 // per) & 1) & ((m0 >> 2) & 1 == (m1 >> 2) & 1)
    q0, q1 = iota((2 * pair, 128), 0), iota((2 * pair, 128), 1)
    q_lane = (q0 // pair) * part + ((q0 % per) // 8) * 4 + (q0 & 3)
    to_q = [onehot(q1 == q_lane + 32 * k).astype(BF16) for k in range(3)]
    s0, s1 = iota((width, 2 * pair), 0), iota((width, 2 * pair), 1)
    slot_half = jnp.where(s1 // pair == 0, h, other)
    to_p = onehot(s0 == slot_half * part + ((s1 % per) // 8) * 4 + (s1 & 3)).astype(BF16)
    o0, o1 = iota((128, 384), 0), iota((128, 384), 1)
    o_q = o0 & 31
    o_slot = o_q >= part
    o_fit = (o_q < 2 * part) & ((o0 // 32) == (o1 // 128))

    def to_out(col, half_of):
        there = jnp.where(o_slot, lax.rem(col + n_col // 2, n_col) * width - part, col * width)
        return onehot(o_fit & ((o1 & 127) == there + half_of * part + o_q)).astype(BF16)

    outs = jnp.concatenate([to_out(c, h), to_out(c, other), to_out(near, h),
                            to_out(near, other)], axis=0)

    def full(main, rest):
        return jnp.concatenate([main, unpack_blocks(rest, main.shape[0] // 16, 16)], axis=1)

    own_right = full(right_main, right_rest)

    for copy in copies:
        copy.wait()
    fold0, fold1 = iota((128, 128), 0), iota((128, 128), 1)
    spread = onehot((fold0 & 15) == (fold1 & 15)).astype(BF16)
    lefts = [jnp.concatenate([left_main, left_rest.astype(BF16)], axis=1)]
    for k in range(3):
        main = lrecv[k, :packed]
        rest = unpack_blocks(lrecv[k, packed:], blocks, 16)
        lefts.append(jnp.concatenate([main, dot(rest, spread).astype(BF16)], axis=1))
    tops = [dot(left[:, :128], to_top).astype(BF16) for left in lefts]

    def stack(parts, t):
        return jnp.concatenate([a[t * pair:(t + 1) * pair] for a in parts], axis=0)

    def nt(a, b):
        return lax.dot_general(a, b, NT, preferred_element_type=F32)

    for copy in bottom_copies:
        copy.wait()
    y_right = jnp.concatenate([full(yrecv[k, :pair], yrecv[k, pair:]) for k in range(2)], axis=0)
    z_right = [unpack_blocks(zrecv[k], blocks, 32) for k in range(2)]
    left_t = [stack(lefts, t) for t in range(3)]
    y_sum = nt(left_t[1], y_right)
    z_sum = sum(nt(stack(tops, t), stack(z_right, t)) for t in range(3))
    w_copy.wait()
    rights = [own_right, full(wrecv[:packed], wrecv[packed:])]
    d_sum = sum(nt(left_t[t], stack(rights, t)) for t in range(3))

    weights = [1.0 / (24.0 * C * C * C), 1.0 / (C * C), 1.0 / (C * C)]
    packed_q = sum(dot_split(jnp.where(same_y, total * weight, 0.0), sel)
                   for total, weight, sel in zip([d_sum, y_sum, z_sum], weights, to_q))
    hi, lo = split(packed_q)
    bsend[1] = dot(to_p, hi[2 * pair:]) + dot(to_p, lo[2 * pair:])
    mine = dot(to_p, hi[:2 * pair]) + dot(to_p, lo[:2 * pair])
    bsend[0] = mine
    last = [remote(bsend.at[min(k, 1)], brecv.at[k], 9 + k, peers[k]) for k in range(3)]
    for copy in last:
        copy.start()
    for copy in last:
        copy.wait()
    every = jnp.concatenate([mine, brecv[0], brecv[1], brecv[2]], axis=1)
    result = dot_split(every, outs)
    n_all = n_col * width
    diag_ref[0] = result[:, :n_all]
    coup_ref[0, 0] = result[:, 128:128 + n_all]
    coup_ref[0, 1] = result[:, 256:256 + n_all]


def solution(mesh):
    sizes = dict(mesh.shape)
    n_elem, n_col, n_pole = sizes["elem"], sizes["col"], sizes["pole"]
    assert n_pole % 2 == 0 and n_col == 4

    def local(basis_seed, potential):
        _, _, _, ext, lanes = basis_seed.shape
        width = lanes // ext
        part = width // 2
        rows = ext * part
        packed = C * part
        pair = 4 * part
        tail = 16 * (-(-packed // 128))
        n_all = width * n_col
        own_cells = basis_seed.shape[1] * ext
        turns = n_pole - 1
        vm = pltpu.VMEM
        return pl.pallas_call(
            functools.partial(kernel, n_elem, n_col, n_pole),
            out_shape=(jax.ShapeDtypeStruct((1, width, n_all), F32),
                       jax.ShapeDtypeStruct((1, 2, width, n_all), F32)),
            in_specs=[pl.BlockSpec(memory_space=pltpu.VMEM)] * 2,
            out_specs=(pl.BlockSpec(memory_space=pltpu.VMEM),) * 2,
            scratch_shapes=[
                vm((turns, rows, own_cells), BF16), vm((turns, rows, own_cells), BF16),
                vm((packed + tail, 128), BF16), vm((3, packed + tail, 128), BF16),
                vm((packed + tail, 128), BF16), vm((packed + tail, 128), BF16),
                vm((pair + 16, 128), BF16), vm((2, pair + 16, 128), BF16),
                vm((48, 128), BF16), vm((2, 48, 128), BF16),
                vm((2, width, 128), F32), vm((3, width, 128), F32),
                pltpu.SemaphoreType.DMA((12 + turns,)), pltpu.SemaphoreType.DMA((12 + turns,)),
            ],
            compiler_params=pltpu.CompilerParams(
                collective_id=0, has_side_effects=True, vmem_limit_bytes=48 * 1024 * 1024),
        )(basis_seed, potential)

    return jax.shard_map(
        local,
        mesh=mesh,
        in_specs=(P("elem", "pole", "col", None, None), P("elem", None, None)),
        out_specs=(P("elem", "col", None), P("elem", None, "col", None)),
        check_vma=False,
    )
```

time: 116 us -> 23.6 us (0.20)
  blocking collectives: 38.5 us -> 0 us
  starting transfers between devices: 21.1 us -> 0 us
  local copies, waits for them, and re-layouts: 23.1 us -> 2.79 us
  Pallas kernels: 0 us -> 19.9 us
  waiting for transfers between devices: 13.9 us -> 0 us
  other arithmetic: 9.63 us -> 0 us
  matrix products: 7 us -> 0 us
  between operations: 2.09 us -> 0.65 us
    all_gather x2 -> x0, blocking collectives: 30 us -> none  [the longest x1 15.6 us: local(): image_piece = lax.all_gather(right_cells, 'col', axis=0, tiled=True)]
    ppermute x20 -> x0, starting transfers between devices: 21.1 us -> none  [the longest x9 12.2 us: extended(): lax.ppermute(lax.slice_in_dim(block, block.shape[dim] - width, None, axis...]
    pallas_call x0 -> x1, Pallas kernels: none -> 19.9 us  [local(): pl.pallas_call(functools.partial(kernel, n_elem, n_col, n_pole), out_shap...]
    ppermute x20 -> x0, waiting for transfers between devices: 13.9 us -> none  [the longest x9 8.01 us: extended(): lax.ppermute(lax.slice_in_dim(block, 0, width, axis=dim), axis, backward)]
    psum x1 -> x0, blocking collectives: 8.54 us -> none  [local(): diag_full, coupling_full = lax.psum((diag_part, coupling_part), 'pole')]
    dot_general x19 -> x0, matrix products: 7 us -> none  [the longest x18 6.68 us: product(): jnp.einsum('abp,kabq->pkq', left_side, right_faces[:, trace_index], prefe...]
    slice x85 -> x0, local copies, waits for them, and re-layouts: 6.32 us -> none  [the longest x18 1.88 us: apply_hamiltonian(): jnp.roll(center, -stride, 2)]
    reshape x6 -> x0, local copies, waits for them, and re-layouts: 6.15 us -> none  [the longest x1 1.76 us: local(): right_faces = trace_piece.reshape(piece_count, 12, rows_dev, C, width_dev)]
  transfers between devices with their start and end apart: 20 -> 0, of which waited for: 14 -> 0; matrix products, arithmetic and copies ran while one was open for 16% -> 0% of each run, Pallas kernels for 0% -> 0%
where the time goes in v1:
time: 23.6 us; the launch traced here: 23.4 us
  Pallas kernels  19.9 us (84%)
  local copies, waits for them, and re-layouts  2.79 us (12%)
  between operations  0.65 us (3%)
    pallas_call x1, Pallas kernels, local(): pl.pallas_call(functools.partial(kernel, n_elem, n_col, n_pole), out_shap...  19.9 us
    unnamed x6, local copies, waits for them, and re-layouts  2.79 us

profile of v1, /device:TPU:0, one launch (start us, length us, event | category | flops | bytes accessed | tf_op | source)
XLA Modules:
  0.0 23.4 jit_solution(423765112875022256)
XLA Ops:
  0.6 0.0 copy-start
  0.6 0.9 %copy-done = bf16[1,8,1,16,384]{4,3,2,1,0:T(8,128)(2,1)S(1)} copy-done((bf16[1,8,1,16,384]{4,3,2,1,0:T(8,128)(2,1)S(1)}, bf16[1,8,1,16,384]{4,3,2,1,0:T(8,128)(2,1)}, u32[]{:S(2)}) %copy-start) | copy-done | bytes 98328
  1.5 0.0 copy-start.1
  1.5 0.7 %copy-done.1 = bf16[1,16,256]{2,1,0:T(8,128)(2,1)S(1)} copy-done((bf16[1,16,256]{2,1,0:T(8,128)(2,1)S(1)}, bf16[1,16,256]{2,1,0:T(8,128)(2,1)}, u32[]{:S(2)}) %copy-start.1) | copy-done | bytes 8216
  2.2 19.9 %shard_map.41 = (f32[1,24,96]{2,1,0:T(8,128)S(1)}, f32[1,2,24,96]{3,2,1,0:T(8,128)S(1)}) custom-call(bf16[1,8,1,16,384]{4,3,2,1,0:T(8,128)(2,1)S(1)} %copy-done, bf16[1,16,256]{2,1,0:T(8,128)(2,1)S(1)} %copy-done.1), custom_call_target="tpu_custom_call" | custom-call | tf_op jit(solution)/shard_map/pallas_call | solution.py:343
  22.2 0.6 %copy.6 = f32[1,24,96]{2,1,0:T(8,128)} copy(f32[1,24,96]{2,1,0:T(8,128)S(1)} %get-tuple-element.4) | data formatting | bytes 18432
  22.8 0.6 %copy.7 = f32[1,2,24,96]{3,2,1,0:T(8,128)} copy(f32[1,2,24,96]{3,2,1,0:T(8,128)S(1)} %get-tuple-element.5) | data formatting | bytes 36864
Async XLA Ops:
  0.6 0.9 %copy-start = (bf16[1,8,1,16,384]{4,3,2,1,0:T(8,128)(2,1)S(1)}, bf16[1,8,1,16,384]{4,3,2,1,0:T(8,128)(2,1)}, u32[]{:S(2)}) copy-start(bf16[1,8,1,16,384]{4,3,2,1,0:T(8,128)(2,1)} %seed_ref.1) | copy-start | bytes 294916
  1.5 0.7 %copy-start.1 = (bf16[1,16,256]{2,1,0:T(8,128)(2,1)S(1)}, bf16[1,16,256]{2,1,0:T(8,128)(2,1)}, u32[]{:S(2)}) copy-start(bf16[1,16,256]{2,1,0:T(8,128)(2,1)} %pot_ref.1) | copy-start | bytes 24580

commit v2 on v1

--- a/solution.py
+++ b/solution.py
@@ -45,9 +45,13 @@
     return pltpu.roll(a.reshape(-1, 8, a.shape[-1]), 4, 1).reshape(a.shape)
 
 
-def kernel(n_elem, n_col, n_pole, seed_ref, pot_ref, diag_ref, coup_ref,
+def kernel(n_elem, n_col, n_pole, seed_ref, pot_ref, out_ref,
            xsend, xrecv, lsend, lrecv, wsend, wrecv, ysend, yrecv, zsend, zrecv,
-           bsend, brecv, send_sem, recv_sem):
+           bsend, brecv, seed_here, pot_here, sel_ref, local_sem, send_sem, recv_sem):
+    seed_copy = pltpu.make_async_copy(seed_ref, seed_here, local_sem.at[0])
+    pot_copy = pltpu.make_async_copy(pot_ref, pot_here, local_sem.at[1])
+    seed_copy.start()
+    pot_copy.start()
     _, rows_dev, _, ext, lanes = seed_ref.shape
     width = lanes // ext
     part = width // 2
@@ -87,25 +91,30 @@
             src_ref=src, dst_ref=dst, send_sem=send_sem.at[sem], recv_sem=recv_sem.at[sem],
             device_id=device, device_id_type=MESH)
 
-    seed = seed_ref[0, :, 0].reshape(own_cells, lanes)
     sel_shape = (half, groups, 8, lanes)
     row_s = iota(sel_shape, 2)
     row_col = (iota(sel_shape, 0) * width + iota(sel_shape, 1) * 4 + (row_s & 3)
                + (row_s >> 2) * (half * width))
     lane = iota(sel_shape, 3)
 
-    def pick(which):
-        sel = onehot(lane == row_col + which * part).reshape(rows, lanes).astype(BF16)
-        return lax.dot_general(sel, seed, NT, preferred_element_type=F32)
-
+    def fill(slot, which):
+        sel_ref[slot] = onehot(lane == row_col + which * part).reshape(rows, lanes).astype(BF16)
+
+    def pick(slot, seed):
+        return lax.dot_general(sel_ref[slot], seed, NT, preferred_element_type=F32)
+
+    fill(0, other)
+    fill(1, h)
+    seed_copy.wait()
+    seed = seed_here[0, :, 0].reshape(own_cells, lanes)
     for k, turn in enumerate(turns):
-        xsend[k] = pick(lax.rem(turn, 2)).astype(BF16)
+        xsend[k] = pick(k % 2, seed).astype(BF16)
     pl.semaphore_wait(barrier, len(greet))
     first_copies = [remote(xsend.at[k], xrecv.at[k], 12 + k, (e, c, turn))
                     for k, turn in enumerate(turns)]
     for copy in first_copies:
         copy.start()
-    own = pick(h)
+    own = pick(1, seed)
 
     i0, i1 = iota((cells, cells), 0), iota((cells, cells), 1)
     same_x = (i0 // ext) == (i1 // ext)
@@ -142,7 +151,8 @@
     rep0, rep1 = iota((128, 128), 0), iota((128, 128), 1)
     to_top = onehot((rep0 < 2 * C) & ((rep1 & 31) == rep0)).astype(BF16)
 
-    pot = pot_ref[0].astype(F32)
+    pot_copy.wait()
+    pot = pot_here[0].astype(F32)
     p_shape = (ext, ext, cells)
     pot_z = jnp.where(iota(p_shape, 2) // ext == iota(p_shape, 1), pot[:, None, :], 0.0)
     v_shape = (half, 8, cells)
@@ -299,13 +309,20 @@
     left_t = [stack(lefts, t) for t in range(3)]
     y_sum = nt(left_t[1], y_right)
     z_sum = sum(nt(stack(tops, t), stack(z_right, t)) for t in range(3))
+    near_sum = sum(nt(left_t[t], own_right[t * pair:(t + 1) * pair]) for t in range(3))
+
+    def to_columns(total, mask, weight, sel):
+        return dot_split(jnp.where(mask, total * weight, 0.0), sel)
+
+    vol_weight, face_weight = 1.0 / (24.0 * C * C * C), 1.0 / (C * C)
+    same_one = same_y[:, :pair]
+    packed_q = (to_columns(y_sum, same_y, face_weight, to_q[1])
+                + to_columns(z_sum, same_y, face_weight, to_q[2])
+                + to_columns(near_sum, same_one, vol_weight, to_q[0][:pair]))
     w_copy.wait()
-    rights = [own_right, full(wrecv[:packed], wrecv[packed:])]
-    d_sum = sum(nt(left_t[t], stack(rights, t)) for t in range(3))
-
-    weights = [1.0 / (24.0 * C * C * C), 1.0 / (C * C), 1.0 / (C * C)]
-    packed_q = sum(dot_split(jnp.where(same_y, total * weight, 0.0), sel)
-                   for total, weight, sel in zip([d_sum, y_sum, z_sum], weights, to_q))
+    far_right = full(wrecv[:packed], wrecv[packed:])
+    far_sum = sum(nt(left_t[t], far_right[t * pair:(t + 1) * pair]) for t in range(3))
+    packed_q = packed_q + to_columns(far_sum, same_one, vol_weight, to_q[0][pair:])
     hi, lo = split(packed_q)
     bsend[1] = dot(to_p, hi[2 * pair:]) + dot(to_p, lo[2 * pair:])
     mine = dot(to_p, hi[:2 * pair]) + dot(to_p, lo[:2 * pair])
@@ -316,11 +333,14 @@
     for copy in last:
         copy.wait()
     every = jnp.concatenate([mine, brecv[0], brecv[1], brecv[2]], axis=1)
-    result = dot_split(every, outs)
-    n_all = n_col * width
-    diag_ref[0] = result[:, :n_all]
-    coup_ref[0, 0] = result[:, 128:128 + n_all]
-    coup_ref[0, 1] = result[:, 256:256 + n_all]
+    out_ref[...] = dot_split(every, outs)
+
+
+def write_out(all_ref, diag_ref, coup_ref):
+    n_all = diag_ref.shape[-1]
+    diag_ref[0] = all_ref[:, :n_all]
+    coup_ref[0, 0] = all_ref[:, 128:128 + n_all]
+    coup_ref[0, 1] = all_ref[:, 256:256 + n_all]
 
 
 def solution(mesh):
@@ -340,12 +360,11 @@
         own_cells = basis_seed.shape[1] * ext
         turns = n_pole - 1
         vm = pltpu.VMEM
-        return pl.pallas_call(
+        whole = pl.pallas_call(
             functools.partial(kernel, n_elem, n_col, n_pole),
-            out_shape=(jax.ShapeDtypeStruct((1, width, n_all), F32),
-                       jax.ShapeDtypeStruct((1, 2, width, n_all), F32)),
-            in_specs=[pl.BlockSpec(memory_space=pltpu.VMEM)] * 2,
-            out_specs=(pl.BlockSpec(memory_space=pltpu.VMEM),) * 2,
+            out_shape=jax.ShapeDtypeStruct((width, 3 * 128), F32),
+            in_specs=[pl.BlockSpec(memory_space=pl.ANY)] * 2,
+            out_specs=pl.BlockSpec(memory_space=pltpu.VMEM),
             scratch_shapes=[
                 vm((turns, rows, own_cells), BF16), vm((turns, rows, own_cells), BF16),
                 vm((packed + tail, 128), BF16), vm((3, packed + tail, 128), BF16),
@@ -353,11 +372,19 @@
                 vm((pair + 16, 128), BF16), vm((2, pair + 16, 128), BF16),
                 vm((48, 128), BF16), vm((2, 48, 128), BF16),
                 vm((2, width, 128), F32), vm((3, width, 128), F32),
+                vm(basis_seed.shape, BF16), vm(potential.shape, BF16), vm((2, rows, lanes), BF16), pltpu.SemaphoreType.DMA((2,)),
                 pltpu.SemaphoreType.DMA((12 + turns,)), pltpu.SemaphoreType.DMA((12 + turns,)),
             ],
             compiler_params=pltpu.CompilerParams(
-                collective_id=0, has_side_effects=True, vmem_limit_bytes=48 * 1024 * 1024),
+                collective_id=0, has_side_effects=True, vmem_limit_bytes=60 * 1024 * 1024),
         )(basis_seed, potential)
+        return pl.pallas_call(
+            write_out,
+            out_shape=(jax.ShapeDtypeStruct((1, width, n_all), F32),
+                       jax.ShapeDtypeStruct((1, 2, width, n_all), F32)),
+            in_specs=[pl.BlockSpec(memory_space=pltpu.VMEM)],
+            out_specs=(pl.BlockSpec(memory_space=pltpu.VMEM),) * 2,
+        )(whole)
 
     return jax.shard_map(
         local,

time: 23.6 us -> 22.9 us (0.970)
  local copies, waits for them, and re-layouts: 2.79 us -> 0 us
  Pallas kernels: 19.9 us -> 22.1 us
    unnamed x6 -> x0, local copies, waits for them, and re-layouts: 2.79 us -> none
    pallas_call x0 -> x1, Pallas kernels: none -> 1.38 us  [local(): pl.pallas_call(write_out, out_shape=(jax.ShapeDtypeStruct((1, width, n_al...]
    pallas_call x1, Pallas kernels: 19.9 us -> 20.7 us  [local(): pl.pallas_call(functools.partial(kernel, n_elem, n_col, n_pole), out_shap...]
where the time goes in v2:
time: 22.9 us; the launch traced here: 22.7 us
  Pallas kernels  22.1 us (97%)
  between operations  0.64 us (3%)
    pallas_call x1, Pallas kernels, local(): pl.pallas_call(functools.partial(kernel, n_elem, n_col, n_pole), out_shap...  20.7 us
    pallas_call x1, Pallas kernels, local(): pl.pallas_call(write_out, out_shape=(jax.ShapeDtypeStruct((1, width, n_al...  1.38 us

profile of v2, /device:TPU:0, one launch (start us, length us, event | category | flops | bytes accessed | tf_op | source)
XLA Modules:
  0.0 22.7 jit_solution(6039232349396251310)
XLA Ops:
  0.6 20.7 %shard_map.41.all_ref = f32[24,384]{1,0:T(8,128)} custom-call(bf16[1,8,1,16,384]{4,3,2,1,0:T(8,128)(2,1)} %seed_ref.1, bf16[1,16,256]{2,1,0:T(8,128)(2,1)} %pot_ref.1), custom_call_target="tpu_custom_call" | custom-call | tf_op jit(solution)/shard_map/pallas_call | solution.py:363
  21.3 1.4 %shard_map.42 = (f32[1,24,96]{2,1,0:T(8,128)}, f32[1,2,24,96]{3,2,1,0:T(8,128)}) custom-call(f32[24,384]{1,0:T(8,128)} %shard_map.41.all_ref), custom_call_target="tpu_custom_call" | custom-call | tf_op jit(solution)/shard_map/pallas_call | solution.py:381
